TPU v7x, 256 devices: a whole 4x4x8 slice. The times are simulated.
256 devices in a mesh: label: 8 (over y_hi, x), dp: 32 (over z, y_lo, core).
Axes of the slice: x: 4, y: 4 (y_hi: 2, y_lo: 2; y = y_hi * 2 + y_lo), z: 8, core: 2. Of those that a mesh axis runs over, the one named last changes fastest.
Arguments:
- queries: bfloat16 [12288, 768], P(('label', 'dp')), may hold values from -6 to 6
- positives: int32 [12288, 8], P(('label', 'dp')), may hold values from 0 to 65535
- row_weight: float32 [12288], P(('label', 'dp')), may hold values from 0.02 to 0.2
- label_weight: bfloat16 [65536, 768], P('label'), may hold values from -0.21875 to 0.21875
Outputs:
- query_grad: float32 [12288, 768], P(('label', 'dp'))
- weight_grad: float32 [65536, 768], P(('label', 'dp'))
All inputs are finite; a program needn't handle non-finite values.
Results may differ from a plain program's by a relative error of at most 0.013.
Values may be sent and summed in bfloat16 or wider, within the bound.
A program may use at most 128 MiB of HBM per device.

v0:
```python
import jax
import jax.numpy as jnp
from jax import lax
from jax.sharding import PartitionSpec as P


def on_device(queries, positives, row_weight, label_weight):
    labels_here = label_weight.shape[0]
    label_ids = lax.axis_index("label") * labels_here + lax.iota(jnp.int32, labels_here)
    piece = (
        lax.all_gather(queries, "label", axis=0, tiled=True),
        lax.all_gather(positives, "label", axis=0, tiled=True),
        lax.all_gather(row_weight.astype(jnp.bfloat16), "label", axis=0, tiled=True).astype(
            jnp.float32
        ),
    )
    logits = lax.dot_general(
        piece[0], label_weight, (((1,), (1,)), ((), ())), preferred_element_type=jnp.float32
    )
    targets = jnp.any(piece[1][:, :, None] == label_ids[None, None, :], axis=1).astype(jnp.float32)
    fresh = (piece[2][:, None] * (jax.nn.sigmoid(logits) - targets)).astype(jnp.bfloat16)
    query_store = piece[0]
    query_part = jnp.dot(fresh, label_weight, preferred_element_type=jnp.float32)
    query_grad = lax.psum_scatter(query_part, "label", scatter_dimension=0, tiled=True)
    weight_part = lax.dot_general(
        fresh, query_store, (((0,), (0,)), ((), ())), preferred_element_type=jnp.float32
    )
    weight_grad = lax.psum_scatter(weight_part, "dp", scatter_dimension=0, tiled=True)
    return (query_grad, weight_grad)


def solution(mesh):
    placed = (
        P(("label", "dp"), None),
        P(("label", "dp"), None),
        P(("label", "dp")),
        P("label", None),
    )
    return jax.shard_map(
        on_device,
        mesh=mesh,
        in_specs=placed,
        out_specs=(P(("label", "dp"), None), P(("label", "dp"), None)),
        check_vma=False,
    )
```

profile of v0, /device:TPU:1, one launch (start us, length us, event | category | flops | bytes accessed | tf_op | source)
XLA Modules:
  0.0 526.5 jit_solution(914849965624124579)
XLA Ops:
  7.2 0.0 reduce-scatter.3.cloned.1.call-start
  7.2 0.7 convert_element_type.12
  7.9 1.3 dynamic-slice
  9.8 0.2 dynamic-update-slice
  10.0 21.4 %all-reduce = bf16[384]{0:T(512)(128)(2,1)S(1)} all-reduce(bf16[384]{0:T(512)(128)(2,1)S(1)} %dynamic-update-slice), channel_id=1, replica_groups=mesh['label'=8,'dp'=32] {'label'}, use_global_device_ids=true, to_apply=%add | all-reduce | flops 384 | bytes 1536
  31.5 27.8 %all-gather = s32[8,48,8]{1,2,0:T(8,128)S(1)} all-gather(s32[1,48,8]{1,2,0:T(8,128)} %bitcast.10), channel_id=1, replica_groups=mesh['label'=8,'dp'=32] {'label'}, dimensions={0}, use_global_device_ids=true | all-gather | bytes 13824 | tf_op jit(solution)/shard_map/all_gather | solution.py:12
  59.3 0.1 copy.12
  59.4 30.8 %all_gather.10 = bf16[384,768]{1,0:T(8,128)(2,1)} all-gather(bf16[48,768]{1,0:T(8,128)(2,1)} %param.4), channel_id=1, replica_groups=mesh['label'=8,'dp'=32] {'label'}, dimensions={0}, use_global_device_ids=true | all-gather | bytes 663552 | tf_op jit(solution)/shard_map/all_gather | solution.py:11
  90.2 36.0 %compare_reduce_fusion = pred[384,8192]{1,0:T(8,128)(4,1)S(1)} fusion(s32[8192]{0:T(1024)S(1)} %iota_add_fusion, s32[384,8]{1,0:T(8,128)S(1)} %bitcast.9), kind=kLoop, calls=%fused_computation | loop fusion | flops 47185920 | bytes 3190784 | tf_op jit(solution)/shard_map/reduce_or | solution.py:20
  126.2 9.5 %multiply_convert_fusion = bf16[384,8192]{1,0:T(8,128)(2,1)S(1)} fusion(pred[384,8192]{1,0:T(8,128)(4,1)S(1)} %compare_reduce_fusion, bf16[384,768]{1,0:T(8,128)(2,1)} %all_gather.10, bf16[8192,768]{1,0:T(8,128)(2,1)} %param.7, f32[384]{0:T(512)S(1)} %convert_element_type.13), kind=kOutput, calls=%fused_computation.1 | convolution fusion | flops 4853858304 | bytes 22611456 | tf_op jit(solution)/shard_map/dot_general | solution.py:17
  135.8 0.0 copy-start
  135.8 2.7 copy-done
  138.5 0.0 copy-start.1
  138.5 9.1 %fusion = f32[384,768]{1,0:T(8,128)} fusion(bf16[384,8192]{1,0:T(8,128)(2,1)S(1)} %multiply_convert_fusion, bf16[8192,768]{1,0:T(8,128)(2,1)} %param.7), kind=kOutput, calls=%fused_computation.3 | convolution fusion | flops 4831838208 | bytes 20054016 | tf_op jit(solution)/shard_map/dot_general | solution.py:23
  147.6 0.0 reduce-scatter.3.cloned.1.call-update
  147.6 0.0 reduce-scatter.5.cloned.1.call-start
  147.7 0.0 copy-done.1
  147.7 14.4 %fusion.1 = f32[8192,768]{1,0:T(8,128)} fusion(bf16[384,8192]{1,0:T(8,128)(2,1)} %copy-done, bf16[384,768]{1,0:T(8,128)(2,1)S(1)} %copy-done.1), kind=kOutput, calls=%fused_computation.4 | convolution fusion | flops 4831838208 | bytes 32047104 | tf_op jit(solution)/shard_map/dot_general | solution.py:25
  162.0 0.0 reduce-scatter.5.cloned.1.call-update
  162.1 77.5 %reduce-scatter.3.cloned.1.call-done = f32[48,768]{1,0:T(8,128)} async-done(((f32[384,768]{1,0:T(8,128)}), f32[48,768]{1,0:T(8,128)}) %reduce-scatter.3.cloned.1.call-update) | async-done | bytes 147472 | tf_op jit(solution)/shard_map/reduce_scatter | solution.py:24
  239.6 280.1 %reduce-scatter.5.cloned.1.call-done = f32[256,768]{1,0:T(8,128)} async-done(((f32[8192,768]{1,0:T(8,128)}), f32[256,768]{1,0:T(8,128)}) %reduce-scatter.5.cloned.1.call-update) | async-done | bytes 786448 | tf_op jit(solution)/shard_map/reduce_scatter | solution.py:28
  (3 shorter events, 0.0 us)
Async XLA Ops:
  7.2 232.4 %reduce-scatter.3.cloned.1.call-start = ((), (), s32[]{:S(2)}) async-start(), calls=%async_computation.2 | async-start | bytes 1327104 | tf_op jit(solution)/shard_map/reduce_scatter | solution.py:24
  135.8 2.7 copy-start
  138.5 9.2 %copy-start.1 = (bf16[384,768]{1,0:T(8,128)(2,1)S(1)}, bf16[384,768]{1,0:T(8,128)(2,1)}, u32[]{:S(2)}) copy-start(bf16[384,768]{1,0:T(8,128)(2,1)} %all_gather.10) | copy-start | bytes 1769476
  147.6 372.1 %reduce-scatter.5.cloned.1.call-start = ((), (), s32[]{:S(2)}) async-start(), calls=%async_computation.3 | async-start | bytes 25952256 | tf_op jit(solution)/shard_map/reduce_scatter | solution.py:28
Sparse Core Ops, SparseCore 0:
  147.7 91.8 reduce-scatter.2
  242.9 276.7 reduce-scatter.4
where the time goes:
time: 527 us
  waiting for transfers between devices  358 us (68%)
  blocking collectives  80.1 us (15%)
  other arithmetic  36.7 us (7%)
  matrix products  33 us (6%)
  between operations  14.7 us (3%)
    reduce_scatter x1, waiting for transfers between devices, on_device(): lax.psum_scatter(weight_part, 'dp', scatter_dimension=0, tiled=True)  280 us
    reduce_scatter x1, waiting for transfers between devices, on_device(): lax.psum_scatter(query_part, 'label', scatter_dimension=0, tiled=True)  77.5 us
    reduce_or x1, other arithmetic, on_device(): jnp.any(piece[1][:, :, None] == label_ids[None, None, :], axis=1)  36 us
    all_gather x1, blocking collectives, on_device(): lax.all_gather(queries, 'label', axis=0, tiled=True)  30.8 us
    all_gather x1, blocking collectives, on_device(): lax.all_gather(positives, 'label', axis=0, tiled=True)  27.8 us
    unnamed x1, blocking collectives  21.4 us
    dot_general x1, matrix products, on_device(): lax.dot_general(fresh, query_store, (((0,), (0,)), ((), ())), preferred_e...  14.4 us
  transfers between devices with their start and end apart: 2, of which 2 were waited for; matrix products, arithmetic and copies ran while one was open for 3% of the time, Pallas kernels for 0%

commit v1 on v0

v1 whole, which is shorter than its diff:
```python
import functools

import jax
import jax.numpy as jnp
from jax import lax
from jax.experimental import pallas as pl
from jax.experimental.pallas import tpu as pltpu
from jax.sharding import PartitionSpec as P

MESH = pl.DeviceIdType.MESH
BF16, F32 = jnp.bfloat16, jnp.float32

ROWS, D, POS = 48, 768, 8
WIDE = D + 128
PLANE = 32 * ROWS
LAB, NZ = 256, 8
HALF = LAB // 2
CUT = 512
COLS = D // 2


def pack_rows(positives, weight_row):
    lane = lax.broadcasted_iota(jnp.int32, (ROWS, 128), 1)
    eye = lax.broadcasted_iota(jnp.int32, (ROWS, ROWS), 0) == lax.broadcasted_iota(
        jnp.int32, (ROWS, ROWS), 1
    )
    weight = jnp.sum(jnp.where(eye, weight_row, 0.0), axis=1, keepdims=True)
    first = weight.astype(BF16).astype(F32)
    rest = weight - first
    second = rest.astype(BF16).astype(F32)
    third = rest - second
    out = jnp.zeros((ROWS, 128), F32)
    for k, part in enumerate((first, second, third)):
        out = jnp.where(lane == 2 * POS + k, part, out)
    for s in range(POS):
        column = positives[:, s : s + 1]
        out = jnp.where(lane == s, (column >> 8).astype(F32), out)
        out = jnp.where(lane == POS + s, (column & 255).astype(F32), out)
    return out.astype(BF16)


def unpack_matrix():
    row = lax.broadcasted_iota(jnp.int32, (16, 128), 0)
    lane = lax.broadcasted_iota(jnp.int32, (16, 128), 1)
    out = jnp.where((lane == row) & (row < POS), 256.0, 0.0)
    out = jnp.where((lane == row + POS) & (row < POS), 1.0, out)
    out = jnp.where((row == POS) & (lane >= 2 * POS) & (lane < 2 * POS + 3), 0.5, out)
    return out.astype(BF16)


def kernel(
    queries,
    positives,
    weight,
    labels,
    query_grad,
    weight_grad,
    q,
    w,
    qg,
    wg,
    g,
    bits,
    half_weight,
    zs,
    zr,
    sib_s,
    sib_r,
    one_s,
    one_r,
    two_s,
    two_r,
    w_sem,
    send_sem,
    recv_sem,
):
    l, d = lax.axis_index("label"), lax.axis_index("dp")
    x, y, z, c = l % 4, (l // 4) * 2 + (d // 2) % 2, d // 4, d % 2
    yc = d % 4
    other = 1 - c
    a, b = jnp.where(c == 0, x, y), jnp.where(c == 0, y, x)

    def device(x, y, z, c):
        return ((y // 2) * 4 + x, z * 4 + (y % 2) * 2 + c)

    def in_plane(a, b):
        return device(jnp.where(c == 0, a, b), jnp.where(c == 0, b, a), z, c)

    def turn(v, k):
        return (v + k + 4) % 4

    a_up, a_down = in_plane(turn(a, 1), b), in_plane(turn(a, -1), b)
    b_up, b_down = in_plane(a, turn(b, 1)), in_plane(a, turn(b, -1))
    z_up, z_down = device(x, y, (z + 1) % 8, c), device(x, y, (z + 7) % 8, c)
    sibling = device(x, y, z, other)

    loads = []
    for k in range(NZ):
        start = pl.multiple_of((k * 4 + yc) * LAB, LAB)
        load = pltpu.make_async_copy(labels.at[pl.ds(start, LAB)], w.at[k], w_sem.at[k])
        load.start()
        loads.append(load)

    barrier = pltpu.get_barrier_semaphore()
    for partner in (a_up, a_down, b_up, b_down, z_up, z_down, sibling):
        pl.semaphore_signal(barrier, inc=1, device_id=partner, device_id_type=MESH)

    def rows_of(cc, bb, aa, count=1):
        return pl.ds(pl.multiple_of(((cc * 4 + bb) * 4 + aa) * ROWS, ROWS), count * ROWS)

    own = rows_of(c, b, a)
    q[own, :D] = queries[...]
    q[own, D:] = pack_rows(positives[...], weight[...])
    pl.semaphore_wait(barrier, 7)

    copies = []

    def send(src, dst, to):
        i = len(copies)
        copy = pltpu.make_async_remote_copy(
            src_ref=src,
            dst_ref=dst,
            send_sem=send_sem.at[i],
            recv_sem=recv_sem.at[i],
            device_id=to,
            device_id_type=MESH,
        )
        copy.start()
        copies.append(copy)
        return copy

    def spread(rows, to, lo=0, hi=WIDE):
        place = q.at[rows, pl.ds(lo, hi - lo)]
        return send(place, place, to)

    order = (0, -1, 1, 2)
    spot = [turn(a, k) for k in order]

    def pieces(bb):
        return [rows_of(c, bb, aa) for aa in spot]

    here, below, above, across = (pieces(turn(b, k)) for k in order)
    up1 = spread(here[0], a_up)
    down1 = spread(here[0], a_down)
    b_up1, b_down1, b_up2, b_down2 = [], [], [], []
    b_up1.append(spread(here[0], b_up))
    b_down1.append(spread(here[0], b_down))
    up1.wait_recv()
    up2 = spread(here[1], a_up, 0, CUT)
    b_up1.append(spread(here[1], b_up))
    b_down1.append(spread(here[1], b_down))
    down1.wait_recv()
    down2 = spread(here[2], a_down, CUT, WIDE)
    b_up1.append(spread(here[2], b_up))
    b_down1.append(spread(here[2], b_down))
    to_sibling = [spread(here[k], sibling) for k in range(3)]
    up2.wait_recv()
    down2.wait_recv()
    b_up1.append(spread(here[3], b_up))
    b_down1.append(spread(here[3], b_down))
    to_sibling.append(spread(here[3], sibling))
    for k in range(4):
        b_up1[k].wait_recv()
        b_up2.append(spread(below[k], b_up, 0, CUT))
        to_sibling.append(spread(below[k], sibling))
        b_down1[k].wait_recv()
        b_down2.append(spread(above[k], b_down, CUT, WIDE))
        to_sibling.append(spread(above[k], sibling))
    qg[...] = jnp.zeros_like(qg)
    for k in range(4):
        b_up2[k].wait_recv()
        b_down2[k].wait_recv()
        to_sibling.append(spread(across[k], sibling))
    for copy in to_sibling:
        copy.wait_recv()
    for load in loads:
        load.wait()

    unpacked = lax.dot_general(
        unpack_matrix(), q[:, D:], (((1,), (1,)), ((), ())), preferred_element_type=F32
    )
    half_weight[...] = jnp.broadcast_to(unpacked[POS : POS + 1], (8, PLANE))
    label = unpacked[:POS].astype(jnp.int32) - l * (4 * NZ * LAB)
    mine = (label >= 0) & (label < 4 * NZ * LAB) & ((label >> 8) % 4 == yc)
    word = jnp.where(mine, (label >> 10) * 8 + (label & 7), -1)
    bit = lax.shift_left(jnp.int32(1), (label >> 3) & 31)
    sub = lax.broadcasted_iota(jnp.int32, (8, PLANE), 0)
    for k in range(NZ):
        held = jnp.zeros((8, PLANE), jnp.int32)
        for s in range(POS):
            held = held | jnp.where(word[s : s + 1] == k * 8 + sub, bit[s : s + 1], 0)
        bits[k] = held

    sent_up, sent_down = [], []

    def pass_on(m, block, first, second):
        for way, (part, half) in enumerate((first, second)):
            rows = pl.ds(half * HALF, HALF)
            total = wg[part, rows, :]
            if m >= 2:
                (sent_up, sent_down)[way][m - 2].wait_recv()
                total = total + zr[way, m - 2].astype(F32)
            zs[way, m] = total.astype(BF16)
            copy = send(zs.at[way, m], zr.at[way, m], (z_up, z_down)[way])
            (sent_up, sent_down)[way].append(copy)

    def compute(j):
        size = 4 - (j + 1) // 2
        plane = (z + jnp.where(j % 2 == 1, size, 8 - size)) % 8
        block = w[plane]
        logits = lax.dot_general(
            block, q[:, :D], (((1,), (1,)), ((), ())), preferred_element_type=F32
        )
        held, scale = bits[plane], half_weight[...]
        parts = []
        for k in range(LAB // 8):
            mask = jnp.int32(1 << k if k < 31 else -(1 << 31))
            target = jnp.where((held & mask) != 0, -1.0, 1.0)
            parts.append(scale * (jnp.tanh(0.5 * logits[8 * k : 8 * k + 8]) + target))
        g[...] = jnp.concatenate(parts, axis=0).astype(BF16)
        qg[...] += lax.dot_general(
            g[...], block, (((0,), (0,)), ((), ())), preferred_element_type=F32
        )
        wg[j] = jnp.dot(g[...], q[:, :D], preferred_element_type=F32)

    def stretch(lo, hi):
        @pl.loop(lo, hi)
        def _(j):
            compute(j)

    stretch(0, 1)
    pass_on(0, 0, (0, 0), (0, 1))
    stretch(1, 3)
    pass_on(1, 1, (1, 1), (2, 0))
    stretch(3, 4)
    pass_on(2, 1, (1, 0), (2, 1))
    stretch(4, 6)
    pass_on(3, 3, (3, 1), (4, 0))
    stretch(6, 8)
    pass_on(4, 3, (3, 0), (4, 1))

    passed = []
    for i, k in enumerate((2, 1, -1, 0)):
        sib_s[i] = qg[rows_of(other, turn(a, k), 0, 4), :].astype(BF16)
        passed.append(send(sib_s.at[i], sib_r.at[i], sibling))
    groups = [rows_of(c, turn(b, k), 0, 4) for k in (2, 1, -1, 0)]
    left, right = slice(0, COLS), slice(COLS, D)

    def ring(group, outgoing, incoming, up, down, prepare, between):
        def start(m, way, block, cols):
            outgoing[way, m] = qg[group[block], cols].astype(outgoing.dtype)
            return send(outgoing.at[way, m], incoming.at[way, m], (up, down)[way])

        def add(copy, m, way, block, cols):
            copy.wait_recv()
            qg[group[block], cols] += incoming[way, m].astype(F32)

        prepare(0)
        up0, down0 = start(0, 0, 0, left), start(0, 1, 0, right)
        prepare(1)
        up1 = start(1, 0, 1, right)
        prepare(2)
        down1 = start(1, 1, 2, left)
        prepare(3)
        between()
        add(up0, 0, 0, 1, left)
        up2 = start(2, 0, 1, left)
        add(down0, 0, 1, 2, right)
        down2 = start(2, 1, 2, right)
        add(up1, 1, 0, 3, right)
        add(down1, 1, 1, 3, left)
        add(up2, 2, 0, 3, left)
        add(down2, 2, 1, 3, right)

    def from_sibling(i):
        passed[i].wait_recv()
        qg[groups[i], :] += sib_r[i].astype(F32)

    ring(
        groups,
        one_s,
        one_r,
        b_up,
        b_down,
        from_sibling,
        lambda: pass_on(5, 5, (5, 1), (6, 0)),
    )
    blocks = [rows_of(c, b, turn(a, k)) for k in (2, 1, -1, 0)]
    ring(
        blocks,
        two_s,
        two_r,
        a_up,
        a_down,
        lambda i: None,
        lambda: pass_on(6, 5, (5, 0), (6, 1)),
    )
    query_grad[...] = qg[own, :]

    low, high = pl.ds(0, HALF), pl.ds(HALF, HALF)
    for m, (up_rows, down_rows) in ((5, (high, low)), (6, (low, high))):
        sent_up[m].wait_recv()
        wg[7, up_rows, :] += zr[0, m].astype(F32)
        sent_down[m].wait_recv()
        wg[7, down_rows, :] += zr[1, m].astype(F32)
    weight_grad[...] = wg[7]

    for copy in copies:
        copy.wait_send()


COPIES = 2 + 8 + 2 + 16 + 8 + 14 + 4 + 6 + 6


def on_device(queries, positives, row_weight, label_weight):
    vmem = pl.BlockSpec(memory_space=pltpu.VMEM)
    return pl.pallas_call(
        kernel,
        out_shape=(
            jax.ShapeDtypeStruct((ROWS, D), F32),
            jax.ShapeDtypeStruct((LAB, D), F32),
        ),
        in_specs=[vmem, vmem, vmem, pl.BlockSpec(memory_space=pl.ANY)],
        out_specs=(vmem, vmem),
        scratch_shapes=[
            pltpu.VMEM((PLANE, WIDE), BF16),
            pltpu.VMEM((NZ, LAB, D), BF16),
            pltpu.VMEM((PLANE, D), F32),
            pltpu.VMEM((NZ, LAB, D), F32),
            pltpu.VMEM((LAB, PLANE), BF16),
            pltpu.VMEM((NZ, 8, PLANE), jnp.int32),
            pltpu.VMEM((8, PLANE), F32),
            pltpu.VMEM((2, 7, HALF, D), BF16),
            pltpu.VMEM((2, 7, HALF, D), BF16),
            pltpu.VMEM((4, 4 * ROWS, D), BF16),
            pltpu.VMEM((4, 4 * ROWS, D), BF16),
            pltpu.VMEM((2, 3, 4 * ROWS, COLS), BF16),
            pltpu.VMEM((2, 3, 4 * ROWS, COLS), BF16),
            pltpu.VMEM((2, 3, ROWS, COLS), F32),
            pltpu.VMEM((2, 3, ROWS, COLS), F32),
            pltpu.SemaphoreType.DMA((NZ,)),
            pltpu.SemaphoreType.DMA((COPIES,)),
            pltpu.SemaphoreType.DMA((COPIES,)),
        ],
        compiler_params=pltpu.CompilerParams(
            collective_id=0, has_side_effects=True, vmem_limit_bytes=56 * 2**20
        ),
        cost_estimate=pl.CostEstimate(
            flops=6 * PLANE * NZ * LAB * D, bytes_accessed=NZ * LAB * D * 2, transcendentals=0
        ),
    )(queries, positives, row_weight[None, :], label_weight)


def solution(mesh):
    placed = (
        P(("label", "dp"), None),
        P(("label", "dp"), None),
        P(("label", "dp")),
        P("label", None),
    )
    return jax.shard_map(
        on_device,
        mesh=mesh,
        in_specs=placed,
        out_specs=(P(("label", "dp"), None), P(("label", "dp"), None)),
        check_vma=False,
    )
```

time: 527 us -> 69.2 us (0.13)
  the two profiles are of different devices: /device:TPU:1 before, /device:TPU:8 now
where the time goes in v1:
time: 69.2 us; the launch traced here: 69 us
  Pallas kernels  63.3 us (91%)
  local copies, waits for them, and re-layouts  5.02 us (7%)
    pallas_call x1, Pallas kernels, on_device(): pl.pallas_call(kernel, out_shape=(jax.ShapeDtypeStruct((ROWS, D), F32), j...  63.3 us
    unnamed x3, local copies, waits for them, and re-layouts  5.02 us

profile of v1, /device:TPU:8, one launch (start us, length us, event | category | flops | bytes accessed | tf_op | source)
XLA Modules:
  0.0 69.0 jit_solution(16096404807440941913)
XLA Ops:
  0.6 1.4 %copy.6.positives = s32[48,8]{1,0:T(8,128)} copy(s32[48,8]{0,1:T(8,128)} %param.5) | data formatting | bytes 3072 | tf_op args[1]
  2.0 63.3 %shard_map.59 = (f32[48,768]{1,0:T(8,128)}, f32[256,768]{1,0:T(8,128)}) custom-call(bf16[48,768]{1,0:T(8,128)(2,1)} %queries.1, s32[48,8]{1,0:T(8,128)} %copy.6.positives, f32[1,48]{1,0:T(1,128)} %bitcast.1, bf16[8192,768]{1,0:T(8,128)(2,1)} %labels.1), custom_call_target="tpu_custom_call" | custom-call | flops 14495514624 | bytes 3145728 | tf_op jit(solution)/shard_map/pallas_call | solution.py:317
  65.3 1.6 %copy.9 = f32[48,768]{1,0:T(8,128)} copy(f32[48,768]{1,0:T(8,128)} %get-tuple-element.4) | data formatting | bytes 294912
  66.9 2.1 %copy.10 = f32[256,768]{1,0:T(8,128)} copy(f32[256,768]{1,0:T(8,128)} %get-tuple-element.5) | data formatting | bytes 1572864

commit v2 on v0

v2 whole, which is shorter than its diff:
```python
import functools

import jax
import jax.numpy as jnp
from jax import lax
from jax.experimental import pallas as pl
from jax.experimental.pallas import tpu as pltpu
from jax.sharding import PartitionSpec as P

MESH = pl.DeviceIdType.MESH
BF16, F32 = jnp.bfloat16, jnp.float32

ROWS, D, POS = 48, 768, 8
PLANE = 32 * ROWS
LAB, NZ = 256, 8
HALF = LAB // 2
CHUNK = 8 * ROWS
RING = (2, 1, -1, 0)
BACK = (0, 2, 1, 3)
HOME = 3
AWAY = (2, -2, 1, -1, 0, 3, -3, 4)


def pack_rows(positives, weight):
    high, low = positives >> 8, positives & 255
    first = weight.astype(BF16).astype(F32)
    rest = weight - first
    second = rest.astype(BF16).astype(F32)
    third = rest - second
    row = lax.broadcasted_iota(jnp.int32, (16, ROWS), 0)
    weights = jnp.where(row == 0, first, jnp.where(row == 1, second, jnp.where(row == 2, third, 0.0)))
    numbers = jnp.concatenate([high, low], axis=0).astype(F32)
    gap = jnp.zeros((16, 16), F32)
    return jnp.concatenate([numbers, gap, weights, gap], axis=1).astype(BF16)


def unpack_rows(packed):
    tiles = [packed[n].astype(F32) for n in range(32)]
    numbers = jnp.concatenate([t[:, :ROWS] for t in tiles], axis=1)
    weights = jnp.concatenate([t[:, 64 : 64 + ROWS] for t in tiles], axis=1)
    ids = (numbers[:POS] * 256.0 + numbers[POS:]).astype(jnp.int32)
    return ids, 0.5 * (weights[0:1] + weights[1:2] + weights[2:3])


def kernel(
    queries,
    positives,
    weight,
    labels,
    query_grad,
    weight_grad,
    q,
    far_q,
    packed,
    far_packed,
    w,
    qg,
    wg,
    g,
    far_g,
    bits,
    half_weight,
    far_bits,
    far_weight,
    my_positives,
    my_weight,
    zs,
    zr,
    sib_s,
    sib_r,
    one_s,
    one_r,
    two_s,
    two_r,
    load_sem,
    send_sem,
    recv_sem,
):
    l, d = lax.axis_index("label"), lax.axis_index("dp")
    x, y, z, c = l % 4, (l // 4) * 2 + (d // 2) % 2, d // 4, d % 2
    yc = d % 4
    a, b = jnp.where(c == 0, x, y), jnp.where(c == 0, y, x)

    def device(x, y, z, c):
        return ((y // 2) * 4 + x, z * 4 + (y % 2) * 2 + c)

    def in_plane(a, b):
        return device(jnp.where(c == 0, a, b), jnp.where(c == 0, b, a), z, c)

    def turn(v, k):
        return (v + k + 4) % 4

    def plane_at(away):
        return (z + jnp.where(c == 0, away + 8, 8 - away)) % 8

    to_a = [in_plane(turn(a, k), b) for k in RING[:3]]
    to_b = [in_plane(a, turn(b, k)) for k in RING[:3]]
    to_z = [device(x, y, plane_at(k), c) for k in (1, -1)]
    opposite = device(x, y, plane_at(4), c)
    sibling = device(x, y, z, 1 - c)

    barrier = pltpu.get_barrier_semaphore()
    for partner in (*to_a, *to_b, *to_z, opposite, sibling):
        pl.semaphore_signal(barrier, inc=1, device_id=partner, device_id_type=MESH)

    def tile(r, h, i):
        return (r * 2 + h) * 4 + i

    def place(r, h, i, count=1):
        return pl.ds(tile(r, h, i) * ROWS, count * ROWS)

    own, own_tile = place(HOME, 0, HOME), tile(HOME, 0, HOME)
    loads = [
        pltpu.make_async_copy(queries, q.at[own], load_sem.at[0]),
        pltpu.make_async_copy(positives, my_positives, load_sem.at[1]),
        pltpu.make_async_copy(weight, my_weight, load_sem.at[2]),
    ]
    for j, away in enumerate(AWAY):
        start = pl.multiple_of((plane_at(away) * 4 + yc) * LAB, LAB)
        loads.append(
            pltpu.make_async_copy(
                labels.at[pl.ds(start, LAB)], w.at[pl.ds(j * LAB, LAB)], load_sem.at[3 + j]
            )
        )
    for load in loads:
        load.start()
    for load in loads[:3]:
        load.wait()
    packed[own_tile] = pack_rows(my_positives[...], my_weight[...])
    pl.semaphore_wait(barrier, 10)

    copies = []

    def prepare(src, dst, to):
        i = len(copies)
        copy = pltpu.make_async_remote_copy(
            src_ref=src,
            dst_ref=dst,
            send_sem=send_sem.at[i],
            recv_sem=recv_sem.at[i],
            device_id=to,
            device_id_type=MESH,
        )
        copies.append(copy)
        return copy

    def send(src, dst, to):
        copy = prepare(src, dst, to)
        copy.start()
        return copy

    def start(group):
        for copy in group:
            copy.start()

    def arrive(group):
        for copy in group:
            copy.wait_recv()

    class Gather:
        def __init__(self, q, packed):
            def rows(src, dst, to):
                return prepare(q.at[place(*src)], q.at[place(*dst)], to)

            def tiles(src, dst, count, to):
                return prepare(
                    packed.at[pl.ds(tile(*src), count)], packed.at[pl.ds(tile(*dst), count)], to
                )

            here = (HOME, 0, HOME)
            self.own_a = [rows(here, (HOME, 0, BACK[r]), to_a[r]) for r in range(3)]
            self.own_tiles = [tiles(here, (HOME, 0, BACK[r]), 1, to_a[r]) for r in range(3)]
            self.to_b = [
                [rows((HOME, 0, i), (BACK[r], 0, i), to_b[r]) for i in range(4)] for r in range(3)
            ]
            self.b_tiles = [tiles((HOME, 0, 0), (BACK[r], 0, 0), 4, to_b[r]) for r in range(3)]
            self.across = [
                [rows((r, 0, i), (r, 1, i), sibling) for i in range(4)] for r in range(4)
            ]
            self.all_tiles = [tiles((r, 0, 0), (r, 1, 0), 4, sibling) for r in range(4)]

        def first(self):
            start(self.own_tiles)
            start(self.own_a)
            for r in (1, 2, 0):
                self.to_b[r][HOME].start()
            self.across[HOME][HOME].start()

        def second(self):
            arrive(self.own_tiles)
            start(self.b_tiles)
            for i in (1, 2, 0):
                self.own_a[BACK[i]].wait_recv()
                self.to_b[1][i].start()
                self.to_b[2][i].start()
                self.across[HOME][i].start()
            for i in (1, 2, 0):
                self.to_b[0][i].start()

        def share_tiles(self):
            arrive(self.b_tiles)
            start(self.all_tiles)

        def share(self, r):
            for i in (3, 1, 2, 0):
                self.to_b[BACK[r]][i].wait_recv()
                self.across[r][i].start()

    near, far = Gather(q, packed), Gather(far_q, far_packed)
    near.first()
    exchange = [
        send(q.at[own], far_q.at[own], opposite),
        send(packed.at[own_tile], far_packed.at[own_tile], opposite),
    ]

    sub = lax.broadcasted_iota(jnp.int32, (8, PLANE), 0)

    def unpack(packed, weights, held, blocks):
        ids, halves = unpack_rows(packed)
        weights[...] = jnp.broadcast_to(halves, (8, PLANE))
        label = ids - l * (4 * NZ * LAB)
        mine = (label >= 0) & (label < 4 * NZ * LAB) & (((label >> 8) & 3) == yc)
        word = jnp.where(mine, (label >> 10) * 8 + (label & 7), -1)
        bit = lax.shift_left(jnp.int32(1), (label >> 3) & 31)
        for n, j in enumerate(blocks):
            words = jnp.zeros((8, PLANE), jnp.int32)
            for s in range(POS):
                hit = word[s : s + 1] == plane_at(AWAY[j]) * 8 + sub
                words = words | jnp.where(hit, bit[s : s + 1], 0)
            held[n] = words

    def block(j, count):
        return pl.ds(j * LAB, count * LAB)

    def gradient(j, count, rows, held, scale):
        logits = lax.dot_general(
            w[block(j, count), :], rows, (((1,), (1,)), ((), ())), preferred_element_type=F32
        )
        parts = []
        for n in range(count):
            for k in range(LAB // 8):
                mask = jnp.int32(1 << k if k < 31 else -(1 << 31))
                target = jnp.where((held[n] & mask) != 0, -1.0, 1.0)
                at = n * LAB + 8 * k
                parts.append(scale * (jnp.tanh(0.5 * logits[at : at + 8]) + target))
        return jnp.concatenate(parts, axis=0).astype(BF16)

    def forward(j, count, rows, first=False):
        held = [bits[j + n, :, rows] for n in range(count)]
        out = g.at[pl.ds(0, count * LAB), rows]
        out[...] = gradient(j, count, q[rows, :], held, half_weight[:, rows])
        part = lax.dot_general(
            out[...], w[block(j, count), :], (((0,), (0,)), ((), ())), preferred_element_type=F32
        )
        if first:
            qg[rows, :] = part
        else:
            qg[rows, :] += part

    def backward(j, count, rows, first):
        part = jnp.dot(g[pl.ds(0, count * LAB), rows], q[rows, :], preferred_element_type=F32)
        if first:
            wg[block(j, count), :] = part
        else:
            wg[block(j, count), :] += part

    def far_backward(j, count):
        out = far_g.at[pl.ds(0, count * LAB)]
        held = [far_bits[j - 2 + n] for n in range(count)]
        out[...] = gradient(j, count, far_q[...], held, far_weight[...])
        wg[block(j, count), :] += jnp.dot(out[...], far_q[...], preferred_element_type=F32)

    everyone = pl.ds(0, PLANE)

    def chunk(r):
        return pl.ds(r * CHUNK, CHUNK)

    near.second()
    arrive(exchange)
    far.first()
    near.share_tiles()
    arrive(near.all_tiles)
    unpack(packed, half_weight, bits, range(8))
    for load in loads[3:]:
        load.wait()
    for n, r in enumerate((HOME, 1, 2, 0)):
        arrive(near.across[r])
        forward(0, 2, chunk(r), first=True)
        backward(0, 2, chunk(r), first=n == 0)
        if n == 0:
            for k in (1, 2, 0):
                near.share(k)
        if n == 2:
            far.second()

    passes = [[prepare(zs.at[t, m], zr.at[t, m], to_z[t]) for m in range(4)] for t in range(2)]

    def pass_on(m, way):
        total = wg[pl.ds((2 * (m // 2) + way) * LAB + m % 2 * HALF, HALF), :]
        if m >= 2:
            passes[way][m - 2].wait_recv()
            total = total + zr[way, m - 2].astype(F32)
        zs[way, m] = total.astype(BF16)
        passes[way][m].start()

    for m in range(2):
        pass_on(m, 0)
        pass_on(m, 1)

    forward(2, 1, everyone)
    backward(2, 1, everyone, first=True)
    forward(3, 1, everyone)
    backward(3, 1, everyone, first=True)

    crossed, along_b, along_a = [], [], []

    def cross(r):
        sib_s[r] = qg[place(r, 1, 0, 4), :].astype(BF16)
        crossed.append(send(sib_s.at[r], sib_r.at[r], sibling))

    def go_b(r):
        crossed[r].wait_recv()
        rows = place(r, 0, 0, 4)
        total = qg[rows, :] + sib_r[r].astype(F32)
        if r == HOME:
            qg[rows, :] = total
        else:
            one_s[r] = total.astype(BF16)
            along_b.append(send(one_s.at[r], one_r.at[r], to_b[r]))

    for r in range(3):
        forward(4, 4, chunk(r))
        cross(r)
        if r > 0:
            go_b(r - 1)
        if r == 0:
            far.share_tiles()
        if r == 1:
            for k in (1, 2, 0):
                far.share(k)
    arrive(far.all_tiles)
    unpack(far_packed, far_weight, far_bits, (2, 3, 4))
    for r in range(4):
        arrive(far.across[r])
    for way in range(2):
        far_backward(2 + way, 1)
        pass_on(2, way)
        pass_on(3, way)
        if way == 0:
            go_b(2)
    forward(4, 4, chunk(HOME))
    cross(HOME)
    backward(4, 1, everyone, first=True)
    far_backward(4, 1)
    go_b(HOME)

    arrive(along_b)
    for i in range(4):
        part = pl.ds(i * ROWS, ROWS)
        total = qg[place(HOME, 0, i), :]
        for r in range(3):
            total = total + one_r[r, part, :].astype(F32)
        if i == HOME:
            query_grad[...] = total
        else:
            two_s[i] = total.astype(BF16)
            along_a.append(send(two_s.at[i], two_r.at[i], to_a[i]))
    for m in (2, 3):
        half = pl.ds((m - 2) * HALF, HALF)
        total = wg[pl.ds(4 * LAB + (m - 2) * HALF, HALF), :]
        for way in range(2):
            passes[way][m].wait_recv()
            total = total + zr[way, m].astype(F32)
        weight_grad[half, :] = total
    for i in range(3):
        along_a[i].wait_recv()
        query_grad[...] += two_r[i].astype(F32)

    for copy in copies:
        copy.wait_send()


COPIES = 2 * 41 + 2 * 3 + 2 + 8 + 4 + 3 + 3


def hand_over(query_in, weight_in, query_out, weight_out):
    query_out[...] = query_in[...]
    weight_out[...] = weight_in[...]


def on_device(queries, positives, row_weight, label_weight):
    vmem = pl.BlockSpec(memory_space=pltpu.VMEM)
    hbm = pl.BlockSpec(memory_space=pl.ANY)
    outs = (jax.ShapeDtypeStruct((ROWS, D), F32), jax.ShapeDtypeStruct((LAB, D), F32))
    grads = pl.pallas_call(
        kernel,
        out_shape=outs,
        in_specs=[hbm, hbm, hbm, hbm],
        out_specs=(vmem, vmem),
        scratch_shapes=[
            pltpu.VMEM((PLANE, D), BF16),
            pltpu.VMEM((PLANE, D), BF16),
            pltpu.VMEM((32, 16, 128), BF16),
            pltpu.VMEM((32, 16, 128), BF16),
            pltpu.VMEM((NZ * LAB, D), BF16),
            pltpu.VMEM((PLANE, D), F32),
            pltpu.VMEM((5 * LAB, D), F32),
            pltpu.VMEM((4 * LAB, PLANE), BF16),
            pltpu.VMEM((2 * LAB, PLANE), BF16),
            pltpu.VMEM((NZ, 8, PLANE), jnp.int32),
            pltpu.VMEM((8, PLANE), F32),
            pltpu.VMEM((3, 8, PLANE), jnp.int32),
            pltpu.VMEM((8, PLANE), F32),
            pltpu.VMEM((POS, ROWS), jnp.int32),
            pltpu.VMEM((1, ROWS), F32),
            pltpu.VMEM((2, 4, HALF, D), BF16),
            pltpu.VMEM((2, 4, HALF, D), BF16),
            pltpu.VMEM((4, 4 * ROWS, D), BF16),
            pltpu.VMEM((4, 4 * ROWS, D), BF16),
            pltpu.VMEM((3, 4 * ROWS, D), BF16),
            pltpu.VMEM((3, 4 * ROWS, D), BF16),
            pltpu.VMEM((3, ROWS, D), BF16),
            pltpu.VMEM((3, ROWS, D), BF16),
            pltpu.SemaphoreType.DMA((NZ + 3,)),
            pltpu.SemaphoreType.DMA((COPIES,)),
            pltpu.SemaphoreType.DMA((COPIES,)),
        ],
        compiler_params=pltpu.CompilerParams(
            collective_id=0, has_side_effects=True, vmem_limit_bytes=56 * 2**20
        ),
        cost_estimate=pl.CostEstimate(
            flops=6 * PLANE * NZ * LAB * D, bytes_accessed=NZ * LAB * D * 2, transcendentals=0
        ),
    )(queries, positives.T, row_weight[None, :], label_weight)
    return pl.pallas_call(
        hand_over,
        out_shape=outs,
        in_specs=[vmem, vmem],
        out_specs=(vmem, vmem),
        compiler_params=pltpu.CompilerParams(vmem_limit_bytes=56 * 2**20),
    )(*grads)


def solution(mesh):
    placed = (
        P(("label", "dp"), None),
        P(("label", "dp"), None),
        P(("label", "dp")),
        P("label", None),
    )
    return jax.shard_map(
        on_device,
        mesh=mesh,
        in_specs=placed,
        out_specs=(P(("label", "dp"), None), P(("label", "dp"), None)),
        check_vma=False,
    )
```

time: 527 us -> 58.5 us (0.11)
  waiting for transfers between devices: 358 us -> 0 us
  blocking collectives: 80.1 us -> 0 us
  Pallas kernels: 0 us -> 57.6 us
  other arithmetic: 36.7 us -> 0 us
  matrix products: 33 us -> 0 us
  between operations: 14.7 us -> 0.64 us
    reduce_scatter x2 -> x0, waiting for transfers between devices: 358 us -> none  [the longest x1 280 us: on_device(): lax.psum_scatter(weight_part, 'dp', scatter_dimension=0, tiled=True)]
    all_gather x2 -> x0, blocking collectives: 58.6 us -> none  [the longest x1 30.8 us: on_device(): lax.all_gather(queries, 'label', axis=0, tiled=True)]
    pallas_call x0 -> x2, Pallas kernels: none -> 57.6 us  [the longest x1 55.5 us: on_device(): pl.pallas_call(kernel, out_shape=outs, in_specs=[hbm, hbm, hbm, hbm], out...]
    reduce_or x1 -> x0, other arithmetic: 36 us -> none  [on_device(): jnp.any(piece[1][:, :, None] == label_ids[None, None, :], axis=1)]
    dot_general x3 -> x0, matrix products: 33 us -> none  [the longest x1 14.4 us: on_device(): lax.dot_general(fresh, query_store, (((0,), (0,)), ((), ())), preferred_e...]
    unnamed x1 -> x0, blocking collectives: 21.4 us -> none
  transfers between devices with their start and end apart: 2 -> 0, of which waited for: 2 -> 0; matrix products, arithmetic and copies ran while one was open for 3% -> 0% of each run, Pallas kernels for 0% -> 0%
where the time goes in v2:
time: 58.5 us; the launch traced here: 58.3 us
  Pallas kernels  57.6 us (98%)
  between operations  0.64 us (1%)
    pallas_call x1, Pallas kernels, on_device(): pl.pallas_call(kernel, out_shape=outs, in_specs=[hbm, hbm, hbm, hbm], out...  55.5 us
    pallas_call x1, Pallas kernels, on_device(): pl.pallas_call(hand_over, out_shape=outs, in_specs=[vmem, vmem], out_spec...  2.16 us

profile of v2, /device:TPU:1, one launch (start us, length us, event | category | flops | bytes accessed | tf_op | source)
XLA Modules:
  0.0 58.3 jit_solution(8671373549110651330)
XLA Ops:
  0.6 55.5 %shard_map.59 = (f32[48,768]{1,0:T(8,128)}, f32[256,768]{1,0:T(8,128)}) custom-call(bf16[48,768]{1,0:T(8,128)(2,1)} %queries.1, s32[8,48]{1,0:T(8,128)} %bitcast.2, f32[1,48]{1,0:T(1,128)} %bitcast.3, bf16[8192,768]{1,0:T(8,128)(2,1)} %labels.1), custom_call_target="tpu_custom_call" | custom-call | flops 14495514624 | bytes 3145728 | tf_op jit(solution)/shard_map/pallas_call | solution.py:395
  56.1 2.2 %shard_map.60 = (f32[48,768]{1,0:T(8,128)}, f32[256,768]{1,0:T(8,128)}) custom-call(f32[48,768]{1,0:T(8,128)} %get-tuple-element.4.query_in, f32[256,768]{1,0:T(8,128)} %get-tuple-element.5.weight_in), custom_call_target="tpu_custom_call" | custom-call | tf_op jit(solution)/shard_map/pallas_call | solution.py:435

commit v3 on v2

--- a/solution.py
+++ b/solution.py
@@ -34,8 +34,8 @@
     return jnp.concatenate([numbers, gap, weights, gap], axis=1).astype(BF16)
 
 
-def unpack_rows(packed):
-    tiles = [packed[n].astype(F32) for n in range(32)]
+def unpack_rows(packed, lo, hi):
+    tiles = [packed[n].astype(F32) for n in range(lo, hi)]
     numbers = jnp.concatenate([t[:, :ROWS] for t in tiles], axis=1)
     weights = jnp.concatenate([t[:, 64 : 64 + ROWS] for t in tiles], axis=1)
     ids = (numbers[:POS] * 256.0 + numbers[POS:]).astype(jnp.int32)
@@ -159,8 +159,8 @@
 
     class Gather:
         def __init__(self, q, packed):
-            def rows(src, dst, to):
-                return prepare(q.at[place(*src)], q.at[place(*dst)], to)
+            def rows(src, dst, count, to):
+                return prepare(q.at[place(*src, count)], q.at[place(*dst, count)], to)
 
             def tiles(src, dst, count, to):
                 return prepare(
@@ -168,43 +168,46 @@
                 )
 
             here = (HOME, 0, HOME)
-            self.own_a = [rows(here, (HOME, 0, BACK[r]), to_a[r]) for r in range(3)]
+            self.own_a = [rows(here, (HOME, 0, BACK[r]), 1, to_a[r]) for r in range(3)]
             self.own_tiles = [tiles(here, (HOME, 0, BACK[r]), 1, to_a[r]) for r in range(3)]
             self.to_b = [
-                [rows((HOME, 0, i), (BACK[r], 0, i), to_b[r]) for i in range(4)] for r in range(3)
+                [rows((HOME, 0, i), (BACK[r], 0, i), n, to_b[r]) for i, n in ((3, 1), (1, 2), (0, 1))]
+                for r in range(3)
             ]
             self.b_tiles = [tiles((HOME, 0, 0), (BACK[r], 0, 0), 4, to_b[r]) for r in range(3)]
-            self.across = [
-                [rows((r, 0, i), (r, 1, i), sibling) for i in range(4)] for r in range(4)
-            ]
+            self.across = [[rows((r, 0, 0), (r, 1, 0), 4, sibling)] for r in range(3)]
+            self.across.append(
+                [rows(here, (HOME, 1, HOME), 1, sibling), rows((HOME, 0, 0), (HOME, 1, 0), 3, sibling)]
+            )
             self.all_tiles = [tiles((r, 0, 0), (r, 1, 0), 4, sibling) for r in range(4)]
 
         def first(self):
             start(self.own_tiles)
             start(self.own_a)
             for r in (1, 2, 0):
-                self.to_b[r][HOME].start()
-            self.across[HOME][HOME].start()
+                self.to_b[r][0].start()
+            self.across[HOME][0].start()
 
         def second(self):
             arrive(self.own_tiles)
+            self.all_tiles[HOME].start()
             start(self.b_tiles)
-            for i in (1, 2, 0):
-                self.own_a[BACK[i]].wait_recv()
-                self.to_b[1][i].start()
-                self.to_b[2][i].start()
-                self.across[HOME][i].start()
-            for i in (1, 2, 0):
-                self.to_b[0][i].start()
+            self.own_a[1].wait_recv()
+            self.own_a[2].wait_recv()
+            for r in (1, 2, 0):
+                self.to_b[r][1].start()
+            self.own_a[0].wait_recv()
+            for r in (1, 2, 0):
+                self.to_b[r][2].start()
+            self.across[HOME][1].start()
 
         def share_tiles(self):
             arrive(self.b_tiles)
-            start(self.all_tiles)
+            start(self.all_tiles[:HOME])
 
         def share(self, r):
-            for i in (3, 1, 2, 0):
-                self.to_b[BACK[r]][i].wait_recv()
-                self.across[r][i].start()
+            arrive(self.to_b[BACK[r]])
+            start(self.across[r])
 
     near, far = Gather(q, packed), Gather(far_q, far_packed)
     near.first()
@@ -213,21 +216,21 @@
         send(packed.at[own_tile], far_packed.at[own_tile], opposite),
     ]
 
-    sub = lax.broadcasted_iota(jnp.int32, (8, PLANE), 0)
-
-    def unpack(packed, weights, held, blocks):
-        ids, halves = unpack_rows(packed)
-        weights[...] = jnp.broadcast_to(halves, (8, PLANE))
+    def unpack(packed, weights, held, blocks, lo, hi):
+        ids, halves = unpack_rows(packed, lo, hi)
+        rows, count = pl.ds(lo * ROWS, (hi - lo) * ROWS), (hi - lo) * ROWS
+        sub = lax.broadcasted_iota(jnp.int32, (8, count), 0)
+        weights[:, rows] = jnp.broadcast_to(halves, (8, count))
         label = ids - l * (4 * NZ * LAB)
         mine = (label >= 0) & (label < 4 * NZ * LAB) & (((label >> 8) & 3) == yc)
         word = jnp.where(mine, (label >> 10) * 8 + (label & 7), -1)
         bit = lax.shift_left(jnp.int32(1), (label >> 3) & 31)
         for n, j in enumerate(blocks):
-            words = jnp.zeros((8, PLANE), jnp.int32)
+            words = jnp.zeros((8, count), jnp.int32)
             for s in range(POS):
                 hit = word[s : s + 1] == plane_at(AWAY[j]) * 8 + sub
                 words = words | jnp.where(hit, bit[s : s + 1], 0)
-            held[n] = words
+            held[n, :, rows] = words
 
     def block(j, count):
         return pl.ds(j * LAB, count * LAB)
@@ -245,9 +248,8 @@
                 parts.append(scale * (jnp.tanh(0.5 * logits[at : at + 8]) + target))
         return jnp.concatenate(parts, axis=0).astype(BF16)
 
-    def forward(j, count, rows, first=False):
+    def forward(j, count, rows, out, first=False):
         held = [bits[j + n, :, rows] for n in range(count)]
-        out = g.at[pl.ds(0, count * LAB), rows]
         out[...] = gradient(j, count, q[rows, :], held, half_weight[:, rows])
         part = lax.dot_general(
             out[...], w[block(j, count), :], (((0,), (0,)), ((), ())), preferred_element_type=F32
@@ -257,8 +259,8 @@
         else:
             qg[rows, :] += part
 
-    def backward(j, count, rows, first):
-        part = jnp.dot(g[pl.ds(0, count * LAB), rows], q[rows, :], preferred_element_type=F32)
+    def backward(j, count, rows, grads, first=False):
+        part = jnp.dot(grads[...], q[rows, :], preferred_element_type=F32)
         if first:
             wg[block(j, count), :] = part
         else:
@@ -270,53 +272,18 @@
         out[...] = gradient(j, count, far_q[...], held, far_weight[...])
         wg[block(j, count), :] += jnp.dot(out[...], far_q[...], preferred_element_type=F32)
 
-    everyone = pl.ds(0, PLANE)
-
     def chunk(r):
         return pl.ds(r * CHUNK, CHUNK)
 
-    near.second()
-    arrive(exchange)
-    far.first()
-    near.share_tiles()
-    arrive(near.all_tiles)
-    unpack(packed, half_weight, bits, range(8))
-    for load in loads[3:]:
-        load.wait()
-    for n, r in enumerate((HOME, 1, 2, 0)):
-        arrive(near.across[r])
-        forward(0, 2, chunk(r), first=True)
-        backward(0, 2, chunk(r), first=n == 0)
-        if n == 0:
-            for k in (1, 2, 0):
-                near.share(k)
-        if n == 2:
-            far.second()
-
-    passes = [[prepare(zs.at[t, m], zr.at[t, m], to_z[t]) for m in range(4)] for t in range(2)]
-
-    def pass_on(m, way):
-        total = wg[pl.ds((2 * (m // 2) + way) * LAB + m % 2 * HALF, HALF), :]
-        if m >= 2:
-            passes[way][m - 2].wait_recv()
-            total = total + zr[way, m - 2].astype(F32)
-        zs[way, m] = total.astype(BF16)
-        passes[way][m].start()
-
-    for m in range(2):
-        pass_on(m, 0)
-        pass_on(m, 1)
-
-    forward(2, 1, everyone)
-    backward(2, 1, everyone, first=True)
-    forward(3, 1, everyone)
-    backward(3, 1, everyone, first=True)
-
-    crossed, along_b, along_a = [], [], []
+    def grads_of(count, rows):
+        return g.at[pl.ds(0, count * LAB), rows]
+
+    others, everyone = pl.ds(0, HOME * CHUNK), pl.ds(0, PLANE)
+    crossed, along_b, along_a = [None] * 4, [], []
 
     def cross(r):
         sib_s[r] = qg[place(r, 1, 0, 4), :].astype(BF16)
-        crossed.append(send(sib_s.at[r], sib_r.at[r], sibling))
+        crossed[r] = send(sib_s.at[r], sib_r.at[r], sibling)
 
     def go_b(r):
         crossed[r].wait_recv()
@@ -328,8 +295,50 @@
             one_s[r] = total.astype(BF16)
             along_b.append(send(one_s.at[r], one_r.at[r], to_b[r]))
 
+    near.second()
+    arrive(exchange)
+    far.first()
+    near.all_tiles[HOME].wait_recv()
+    unpack(packed, half_weight, bits, range(8), 24, 32)
+    for load in loads[3:]:
+        load.wait()
+    arrive(near.across[HOME])
+    forward(0, 4, chunk(HOME), grads_of(4, chunk(HOME)), first=True)
+    backward(0, 4, chunk(HOME), grads_of(4, chunk(HOME)), first=True)
+    near.share_tiles()
+    near.share(1)
+    near.share(2)
+    arrive(near.all_tiles[:HOME])
+    unpack(packed, half_weight, bits, range(8), 0, 24)
+    for r in (1, 2, 0):
+        if r == 2:
+            near.share(0)
+            far.second()
+        arrive(near.across[r])
+        grads = grads_of(2, chunk(r))
+        forward(0, 2, chunk(r), grads, first=True)
+        backward(0, 2, chunk(r), grads)
+
+    passes = [[prepare(zs.at[t, m], zr.at[t, m], to_z[t]) for m in range(4)] for t in range(2)]
+
+    def pass_on(m, way):
+        total = wg[pl.ds((2 * (m // 2) + way) * LAB + m % 2 * HALF, HALF), :]
+        if m >= 2:
+            passes[way][m - 2].wait_recv()
+            total = total + zr[way, m - 2].astype(F32)
+        zs[way, m] = total.astype(BF16)
+        passes[way][m].start()
+
+    for m in range(2):
+        pass_on(m, 0)
+        pass_on(m, 1)
+
+    for j in (2, 3):
+        forward(j, 1, others, grads_of(1, others))
+        backward(j, 1, others, grads_of(1, others))
+
     for r in range(3):
-        forward(4, 4, chunk(r))
+        forward(4, 4, chunk(r), grads_of(4, chunk(r)))
         cross(r)
         if r > 0:
             go_b(r - 1)
@@ -339,7 +348,7 @@
             for k in (1, 2, 0):
                 far.share(k)
     arrive(far.all_tiles)
-    unpack(far_packed, far_weight, far_bits, (2, 3, 4))
+    unpack(far_packed, far_weight, far_bits, (2, 3, 4), 0, 32)
     for r in range(4):
         arrive(far.across[r])
     for way in range(2):
@@ -348,12 +357,13 @@
         pass_on(3, way)
         if way == 0:
             go_b(2)
-    forward(4, 4, chunk(HOME))
+    forward(4, 4, chunk(HOME), grads_of(4, chunk(HOME)))
     cross(HOME)
-    backward(4, 1, everyone, first=True)
-    far_backward(4, 1)
+    backward(4, 1, everyone, grads_of(1, everyone), first=True)
     go_b(HOME)
 
+    for copy in copies[:GATHERED]:
+        copy.wait_send()
     arrive(along_b)
     for i in range(4):
         part = pl.ds(i * ROWS, ROWS)
@@ -365,6 +375,7 @@
         else:
             two_s[i] = total.astype(BF16)
             along_a.append(send(two_s.at[i], two_r.at[i], to_a[i]))
+    far_backward(4, 1)
     for m in (2, 3):
         half = pl.ds((m - 2) * HALF, HALF)
         total = wg[pl.ds(4 * LAB + (m - 2) * HALF, HALF), :]
@@ -376,11 +387,12 @@
         along_a[i].wait_recv()
         query_grad[...] += two_r[i].astype(F32)
 
-    for copy in copies:
+    for copy in copies[GATHERED:]:
         copy.wait_send()
 
 
-COPIES = 2 * 41 + 2 * 3 + 2 + 8 + 4 + 3 + 3
+GATHERED = 2 * 27 + 2
+COPIES = GATHERED + 8 + 4 + 3 + 3
 
 
 def hand_over(query_in, weight_in, query_out, weight_out):
@@ -406,7 +418,7 @@
             pltpu.VMEM((PLANE, D), F32),
             pltpu.VMEM((5 * LAB, D), F32),
             pltpu.VMEM((4 * LAB, PLANE), BF16),
-            pltpu.VMEM((2 * LAB, PLANE), BF16),
+            pltpu.VMEM((LAB, PLANE), BF16),
             pltpu.VMEM((NZ, 8, PLANE), jnp.int32),
             pltpu.VMEM((8, PLANE), F32),
             pltpu.VMEM((3, 8, PLANE), jnp.int32),

time: 58.5 us -> 56.2 us (0.961)
  Pallas kernels: 57.6 us -> 55.5 us
    pallas_call x1, Pallas kernels: 55.5 us -> 53.3 us  [on_device(): pl.pallas_call(kernel, out_shape=outs, in_specs=[hbm, hbm, hbm, hbm], out...]
where the time goes in v3:
time: 56.2 us; the launch traced here: 56.1 us
  Pallas kernels  55.5 us (99%)
  between operations  0.64 us (1%)
    pallas_call x1, Pallas kernels, on_device(): pl.pallas_call(kernel, out_shape=outs, in_specs=[hbm, hbm, hbm, hbm], out...  53.3 us
    pallas_call x1, Pallas kernels, on_device(): pl.pallas_call(hand_over, out_shape=outs, in_specs=[vmem, vmem], out_spec...  2.16 us

profile of v3, /device:TPU:1, one launch (start us, length us, event | category | flops | bytes accessed | tf_op | source)
XLA Modules:
  0.0 56.1 jit_solution(2086354259402672838)
XLA Ops:
  0.6 53.3 %shard_map.59 = (f32[48,768]{1,0:T(8,128)}, f32[256,768]{1,0:T(8,128)}) custom-call(bf16[48,768]{1,0:T(8,128)(2,1)} %queries.1, s32[8,48]{1,0:T(8,128)} %bitcast.2, f32[1,48]{1,0:T(1,128)} %bitcast.3, bf16[8192,768]{1,0:T(8,128)(2,1)} %labels.1), custom_call_target="tpu_custom_call" | custom-call | flops 14495514624 | bytes 3145728 | tf_op jit(solution)/shard_map/pallas_call | solution.py:407
  54.0 2.2 %shard_map.60 = (f32[48,768]{1,0:T(8,128)}, f32[256,768]{1,0:T(8,128)}) custom-call(f32[48,768]{1,0:T(8,128)} %get-tuple-element.4.query_in, f32[256,768]{1,0:T(8,128)} %get-tuple-element.5.weight_in), custom_call_target="tpu_custom_call" | custom-call | tf_op jit(solution)/shard_map/pallas_call | solution.py:447

commit v4 on v3

--- a/solution.py
+++ b/solution.py
@@ -47,8 +47,11 @@
     positives,
     weight,
     labels,
+    query_out,
+    weight_out,
     query_grad,
     weight_grad,
+    out_sem,
     q,
     far_q,
     packed,
@@ -376,6 +379,7 @@
             two_s[i] = total.astype(BF16)
             along_a.append(send(two_s.at[i], two_r.at[i], to_a[i]))
     far_backward(4, 1)
+    stores = []
     for m in (2, 3):
         half = pl.ds((m - 2) * HALF, HALF)
         total = wg[pl.ds(4 * LAB + (m - 2) * HALF, HALF), :]
@@ -383,12 +387,18 @@
             passes[way][m].wait_recv()
             total = total + zr[way, m].astype(F32)
         weight_grad[half, :] = total
+        stores.append(pltpu.make_async_copy(weight_grad.at[half], weight_out.at[half], out_sem.at[m - 2]))
+        stores[-1].start()
     for i in range(3):
         along_a[i].wait_recv()
         query_grad[...] += two_r[i].astype(F32)
+    stores.append(pltpu.make_async_copy(query_grad, query_out, out_sem.at[2]))
+    stores[-1].start()
 
     for copy in copies[GATHERED:]:
         copy.wait_send()
+    for store in stores:
+        store.wait()
 
 
 GATHERED = 2 * 27 + 2
@@ -408,8 +418,11 @@
         kernel,
         out_shape=outs,
         in_specs=[hbm, hbm, hbm, hbm],
-        out_specs=(vmem, vmem),
+        out_specs=(hbm, hbm),
         scratch_shapes=[
+            pltpu.VMEM((ROWS, D), F32),
+            pltpu.VMEM((LAB, D), F32),
+            pltpu.SemaphoreType.DMA((3,)),
             pltpu.VMEM((PLANE, D), BF16),
             pltpu.VMEM((PLANE, D), BF16),
             pltpu.VMEM((32, 16, 128), BF16),

time: 56.2 us -> 56.1 us (level)
  no operation moved by 1% of the time
where the time goes in v4:
time: 56.1 us; the launch traced here: 56 us
  Pallas kernels  55.3 us (99%)
  between operations  0.64 us (1%)
    pallas_call x1, Pallas kernels, on_device(): pl.pallas_call(kernel, out_shape=outs, in_specs=[hbm, hbm, hbm, hbm], out...  53.2 us
    pallas_call x1, Pallas kernels, on_device(): pl.pallas_call(hand_over, out_shape=outs, in_specs=[vmem, vmem], out_spec...  2.16 us

profile of v4, /device:TPU:1, one launch (start us, length us, event | category | flops | bytes accessed | tf_op | source)
XLA Modules:
  0.0 56.0 jit_solution(1295026041782034795)
XLA Ops:
  0.6 53.2 %shard_map.59 = (f32[48,768]{1,0:T(8,128)}, f32[256,768]{1,0:T(8,128)}) custom-call(bf16[48,768]{1,0:T(8,128)(2,1)} %queries.1, s32[8,48]{1,0:T(8,128)} %bitcast.2, f32[1,48]{1,0:T(1,128)} %bitcast.3, bf16[8192,768]{1,0:T(8,128)(2,1)} %labels.1), custom_call_target="tpu_custom_call" | custom-call | flops 14495514624 | bytes 3145728 | tf_op jit(solution)/shard_map/pallas_call | solution.py:417
  53.8 2.2 %shard_map.60 = (f32[48,768]{1,0:T(8,128)}, f32[256,768]{1,0:T(8,128)}) custom-call(f32[48,768]{1,0:T(8,128)} %get-tuple-element.4.query_in, f32[256,768]{1,0:T(8,128)} %get-tuple-element.5.weight_in), custom_call_target="tpu_custom_call" | custom-call | tf_op jit(solution)/shard_map/pallas_call | solution.py:460
